TPU v7x, 512 devices: a whole 4x8x8 slice. The times are simulated.
512 devices in a mesh: dp: 128 (over z, y, core), rep: 4 (over x).
Axes of the slice: x: 4, y: 8, z: 8, core: 2. Of those that a mesh axis runs over, the one named last changes fastest.
Arguments:
- tokens: bfloat16 [8192, 2048], P(('dp', 'rep')), may hold values from -6 to 6
- norm_gain: float32 [2048], replicated, may hold values from 0.1 to 1.9
- expert_weights: bfloat16 [64, 2048, 2304], P(None, ('dp', 'rep')), may hold values from -0.125 to 0.125
- slot_expert: int32 [128], replicated, may hold values from 0 to 63, as said below
- pair_slots: int32 [8192, 8], P(('dp', 'rep')), may hold values from 0 to 127, all different within a row; in each aligned block of 16 rows (0 to 15, 16 to 31, ...) at most 2 rows name the same one
- combine_weights: float32 [8192, 8], P(('dp', 'rep')), may hold values from 0.25 to 2
Outputs:
- layer_out: bfloat16 [8192, 2048], P(('dp', 'rep'))
Inputs may be any that keep to these rules, and one draw needn't show every extreme that they name: `slot_expert`: every one of the 64 experts is held by at least one slot. `pair_slots`: each row names 8 different slots; among the 16 rows of one device no slot is named by more than 2 rows.
All inputs are finite; a program needn't handle non-finite values.
Results may differ from a plain program's by a relative error of at most 0.0071.
Values may be sent and summed in bfloat16 or wider, within the bound.
A program may use at most 64 MiB of HBM per device.

v0:
```python
import jax
import jax.numpy as jnp
from jax import lax
from jax.sharding import PartitionSpec as P


def per_device(tokens, norm_gain, expert_weights, slot_expert, pair_slots, combine_weights):
    slot_count = lax.axis_size("dp")
    model_width = tokens.shape[1]
    packed_width = expert_weights.shape[2]
    hidden_units = packed_width // 3
    token_count = tokens.shape[0]
    choice_count = pair_slots.shape[1]
    pair_count = token_count * choice_count
    capacity = max(2, 2 * pair_count // slot_count)
    blocks = lax.all_gather(expert_weights, "rep", axis=1, tiled=True)
    outgoing = jnp.take(blocks, slot_expert, axis=0)
    arrived = lax.all_to_all(outgoing, "dp", split_axis=0, concat_axis=0, tiled=True)
    weight = arrived.reshape(model_width, packed_width)
    values = tokens.astype(jnp.float32)
    mean_square = jnp.mean(values * values, axis=1, keepdims=True)
    normed = (values * lax.rsqrt(mean_square + 1e-06) * norm_gain[None, :]).astype(jnp.bfloat16)
    targets = pair_slots.reshape(pair_count)
    onehot = (targets[:, None] == jnp.arange(slot_count, dtype=jnp.int32)[None, :]).astype(
        jnp.int32
    )
    before = jnp.cumsum(onehot, axis=0) - onehot
    position = jnp.sum(before * onehot, axis=1)
    target_row = targets * capacity + position
    selector = (
        jnp.arange(slot_count * capacity, dtype=jnp.int32)[:, None] == target_row[None, :]
    ).astype(jnp.bfloat16)
    pair_rows = jnp.repeat(normed, choice_count, axis=0)
    outbound = jnp.dot(selector, pair_rows, preferred_element_type=jnp.float32).astype(jnp.bfloat16)
    outbound = outbound.reshape(slot_count, capacity, model_width)
    rows = lax.all_to_all(outbound, "dp", split_axis=0, concat_axis=0, tiled=True).reshape(
        -1, model_width
    )
    gate_up = jnp.dot(rows, weight[:, : 2 * hidden_units], preferred_element_type=jnp.float32)
    hidden = (jax.nn.silu(gate_up[:, :hidden_units]) * gate_up[:, hidden_units:]).astype(
        jnp.bfloat16
    )
    result = lax.dot_general(
        hidden,
        weight[:, 2 * hidden_units :],
        (((1,), (1,)), ((), ())),
        preferred_element_type=jnp.float32,
    )
    result = result.astype(jnp.bfloat16).reshape(slot_count, -1, model_width)
    returned = lax.all_to_all(result, "dp", split_axis=0, concat_axis=0, tiled=True)
    expert_out = jnp.dot(
        selector.T,
        returned.reshape(slot_count * capacity, model_width),
        preferred_element_type=jnp.float32,
    )
    expert_out = expert_out.reshape(token_count, choice_count, model_width)
    mixed = jnp.sum(expert_out * combine_weights[:, :, None], axis=1)
    return mixed.astype(jnp.bfloat16)


def solution(mesh):
    placed = (
        P(("dp", "rep"), None),
        P(),
        P(None, ("dp", "rep"), None),
        P(),
        P(("dp", "rep"), None),
        P(("dp", "rep"), None),
    )
    return jax.shard_map(
        per_device, mesh=mesh, in_specs=placed, out_specs=P(("dp", "rep"), None), check_vma=False
    )
```

profile of v0, /device:TPU:6, one launch (start us, length us, event | category | flops | bytes accessed | tf_op | source)
XLA Modules:
  0.0 459.1 jit_solution(11894909106888529398)
XLA Ops:
  6.5 0.0 copy-start.1
  6.5 0.0 all-gather.2.cloned.1.call-start
  6.5 2.5 copy.15
  9.0 0.0 all-gather.2.cloned.1.call-update
  9.0 0.8 copy.14
  9.8 0.1 reshape.71
  9.9 0.1 fusion.20
  10.0 0.2 reduce_window_sum.11
  10.1 1.0 fusion.13
  11.1 0.2 select_reduce_fusion
  11.3 0.9 fusion.15
  12.2 0.4 convolution_convert_fusion
  12.7 1.5 reshape.73
  14.2 17.8 %all-to-all-start = ((bf16[128,2,2048]{2,1,0:T(2,128)(2,1)}), bf16[128,2,2048]{2,1,0:T(2,128)(2,1)S(1)}, u32[]{:S(2)}, u32[]{:S(2)}) async-start(bf16[128,2,2048]{2,1,0:T(2,128)(2,1)} %reshape.73), calls=%async_computation | async-start | bytes 2097152 | tf_op jit(solution)/shard_map/all_to_all | solution.py:36
  32.0 0.0 copy-done.1
  32.0 38.3 %all-gather.2.cloned.1.call-done = bf16[64,16,2304]{2,0,1:T(8,128)(2,1)} async-done(((bf16[64,4,2304]{2,0,1:T(8,128)(2,1)}), bf16[64,16,2304]{2,0,1:T(8,128)(2,1)}) %all-gather.2.cloned.1.call-update) | async-done | bytes 4718608 | tf_op jit(solution)/shard_map/all_gather | solution.py:16
  70.3 7.1 %copy.16 = bf16[64,16,2304]{2,1,0:T(8,128)(2,1)} copy(bf16[64,16,2304]{2,0,1:T(8,128)(2,1)} %all-gather.2.cloned.1.call-done) | data formatting | bytes 9437184 | tf_op jit(solution)/shard_map/all_gather | solution.py:16
  77.4 9.6 %gather_fusion = bf16[128,16,2304]{2,1,0:T(8,128)(2,1)} fusion(bf16[64,16,2304]{2,1,0:T(8,128)(2,1)} %copy.16, s32[1024]{0:T(1024)S(1)} %pad_clamp_fusion), kind=kCustom, calls=%fused_computation | custom fusion | bytes 18874880 | tf_op jit(solution)/shard_map/jit(_take)/gather | solution.py:17
  87.0 8.2 %broadcast_select_fusion = bf16[128,16,2304]{2,1,0:T(8,128)(2,1)} fusion(bf16[128,16,2304]{2,1,0:T(8,128)(2,1)} %gather_fusion, pred[128]{0:T(512)(128)(4,1)S(1)} %compare_and_fusion), kind=kLoop, calls=%fused_computation.1 | loop fusion | flops 4718592 | bytes 18874496 | tf_op jit(solution)/shard_map/jit(_take)/select_n | solution.py:17
  95.2 0.0 all-to-all-done
  95.2 15.4 %all-to-all-start.1 = ((bf16[128,16,2304]{2,1,0:T(8,128)(2,1)}), bf16[128,16,2304]{2,1,0:T(8,128)(2,1)}, u32[]{:S(2)}, u32[]{:S(2)}) async-start(bf16[128,16,2304]{2,1,0:T(8,128)(2,1)} %broadcast_select_fusion), calls=%async_computation.1 | async-start | bytes 18874368 | tf_op jit(solution)/shard_map/all_to_all | solution.py:18
  110.6 0.4 reshape.74
  111.1 260.1 %all-to-all-done.1 = bf16[128,16,2304]{2,1,0:T(8,128)(2,1)} async-done(((bf16[128,16,2304]{2,1,0:T(8,128)(2,1)}), bf16[128,16,2304]{2,1,0:T(8,128)(2,1)}, u32[]{:S(2)}, u32[]{:S(2)}) %all-to-all-start.1) | async-done | bytes 9437216 | tf_op jit(solution)/shard_map/all_to_all | solution.py:18
  371.1 4.6 fusion
  375.7 0.0 copy-start
  375.7 2.9 fusion.4
  378.7 1.5 reshape.76
  380.2 40.3 %all-to-all-start.2 = ((bf16[128,2,2048]{2,1,0:T(2,128)(2,1)}), bf16[128,2,2048]{2,1,0:T(2,128)(2,1)S(1)}, u32[]{:S(2)}, u32[]{:S(2)}) async-start(bf16[128,2,2048]{2,1,0:T(2,128)(2,1)} %reshape.76), calls=%async_computation.2 | async-start | bytes 2097152 | tf_op jit(solution)/shard_map/all_to_all | solution.py:50
  420.4 0.0 copy-done
  420.4 0.1 copy.17
  420.5 30.2 %all-to-all-done.2 = bf16[128,2,2048]{2,1,0:T(2,128)(2,1)S(1)} async-done(((bf16[128,2,2048]{2,1,0:T(2,128)(2,1)}), bf16[128,2,2048]{2,1,0:T(2,128)(2,1)S(1)}, u32[]{:S(2)}, u32[]{:S(2)}) %all-to-all-start.2) | async-done | bytes 1048608 | tf_op jit(solution)/shard_map/all_to_all | solution.py:50
  450.7 0.4 reshape.87
  451.2 1.1 fusion.7
  (5 shorter events, 0.0 us)
Async XLA Ops:
  6.5 25.5 %copy-start.1 = (s32[128]{0:T(128)S(1)}, s32[128]{0:T(128)}, u32[]{:S(2)}) copy-start(s32[128]{0:T(128)} %param.9) | copy-start | bytes 1540
  6.5 63.8 %all-gather.2.cloned.1.call-start = ((), (), s32[]{:S(2)}) async-start(), calls=%async_computation.3 | async-start | bytes 5898240 | tf_op jit(solution)/shard_map/all_gather | solution.py:16
  14.2 81.0 %all-to-all-start = ((bf16[128,2,2048]{2,1,0:T(2,128)(2,1)}), bf16[128,2,2048]{2,1,0:T(2,128)(2,1)S(1)}, u32[]{:S(2)}, u32[]{:S(2)}) async-start(bf16[128,2,2048]{2,1,0:T(2,128)(2,1)} %reshape.73), calls=%async_computation | async-start | bytes 2097152 | tf_op jit(solution)/shard_map/all_to_all | solution.py:36
  95.2 275.9 %all-to-all-start.1 = ((bf16[128,16,2304]{2,1,0:T(8,128)(2,1)}), bf16[128,16,2304]{2,1,0:T(8,128)(2,1)}, u32[]{:S(2)}, u32[]{:S(2)}) async-start(bf16[128,16,2304]{2,1,0:T(8,128)(2,1)} %broadcast_select_fusion), calls=%async_computation.1 | async-start | bytes 18874368 | tf_op jit(solution)/shard_map/all_to_all | solution.py:18
  375.7 44.7 %copy-start = (f32[16,8]{0,1:T(8,128)S(1)}, f32[16,8]{0,1:T(8,128)}, u32[]{:S(2)}) copy-start(f32[16,8]{0,1:T(8,128)} %param.11) | copy-start | bytes 1540
  380.2 70.6 %all-to-all-start.2 = ((bf16[128,2,2048]{2,1,0:T(2,128)(2,1)}), bf16[128,2,2048]{2,1,0:T(2,128)(2,1)S(1)}, u32[]{:S(2)}, u32[]{:S(2)}) async-start(bf16[128,2,2048]{2,1,0:T(2,128)(2,1)} %reshape.76), calls=%async_computation.2 | async-start | bytes 2097152 | tf_op jit(solution)/shard_map/all_to_all | solution.py:50
Sparse Core Ops, SparseCore 0:
  9.5 60.8 all-gather.1
where the time goes:
time: 463 us; the launch traced here: 459 us
  waiting for transfers between devices  329 us (71%)
  starting transfers between devices  73.5 us (16%)
  local copies, waits for them, and re-layouts  23.9 us (5%)
  between operations  13.5 us (3%)
  other arithmetic  10.6 us (2%)
  matrix products  9.05 us (2%)
    all_to_all x1, waiting for transfers between devices, per_device(): lax.all_to_all(outgoing, 'dp', split_axis=0, concat_axis=0, tiled=True)  260 us
    all_to_all x1, starting transfers between devices, per_device(): lax.all_to_all(result, 'dp', split_axis=0, concat_axis=0, tiled=True)  40.3 us
    all_gather x1, waiting for transfers between devices, per_device(): blocks = lax.all_gather(expert_weights, 'rep', axis=1, tiled=True)  38.3 us
    all_to_all x1, waiting for transfers between devices, per_device(): lax.all_to_all(result, 'dp', split_axis=0, concat_axis=0, tiled=True)  30.2 us
    all_to_all x1, starting transfers between devices, per_device(): lax.all_to_all(outbound, 'dp', split_axis=0, concat_axis=0, tiled=True)  17.8 us
    all_to_all x1, starting transfers between devices, per_device(): lax.all_to_all(outgoing, 'dp', split_axis=0, concat_axis=0, tiled=True)  15.4 us
    gather x1, local copies, waits for them, and re-layouts, per_device(): outgoing = jnp.take(blocks, slot_expert, axis=0)  9.57 us
  transfers between devices with their start and end apart: 4, of which 3 were waited for; matrix products, arithmetic and copies ran while one was open for 7% of the time, Pallas kernels for 0%

commit v1 on v0

v1 whole, which is shorter than its diff:
```python
import jax
import jax.numpy as jnp
from jax import lax
from jax.experimental import pallas as pl
from jax.experimental.pallas import tpu as pltpu
from jax.sharding import PartitionSpec as P

NZ, NY, NX = 8, 8, 4
D, F, ROWS = 2048, 768, 16
HALF = D // 2
TILES = 3 * F // 128
BF16, F32 = jnp.bfloat16, jnp.float32


def mod(value, size):
    return lax.rem(value + 2 * size, size)


def kernel(tok_ref, gain_ref, w_ref, slot_ref, pair_ref, comb_ref, out_ref,
           xa, xb, wraw, wmat, acc, hid, coef, rs_send, rs_recv, fin_send, fin_recv,
           sem_a1, sem_b1, sem_s1, ring_r, ring_s, w_recv, w_send, w_own,
           x_recv, x_send, f_recv, f_send, c_recv, c_send,
           rs_r, rs_s, fin_r, fin_s):
    dp, x = lax.axis_index("dp"), lax.axis_index("rep")
    z, y, core = dp // (2 * NY), lax.rem(dp // 2, NY), lax.rem(dp, 2)

    def at(zz, yy):
        return (zz * (2 * NY) + yy * 2 + core, x)

    def move(src, dst, send, recv, device):
        return pltpu.make_async_remote_copy(
            src_ref=src, dst_ref=dst, send_sem=send, recv_sem=recv,
            device_id=device, device_id_type=pl.DeviceIdType.MESH)

    right, left = (dp, mod(x + 1, NX)), (dp, mod(x - 1, NX))
    other = (dp + 1 - 2 * core, x)

    barrier = pltpu.get_barrier_semaphore()

    def greet(i, _):
        pl.semaphore_signal(barrier, inc=1, device_id=at(mod(z + i // NY, NZ), mod(y + lax.rem(i, NY), NY)),
                            device_id_type=pl.DeviceIdType.MESH)
        return 0

    lax.fori_loop(1, NZ * NY, greet, 0)
    for device in (right, left, other):
        pl.semaphore_signal(barrier, inc=1, device_id=device, device_id_type=pl.DeviceIdType.MESH)

    values = tok_ref[...].astype(F32)
    mean_square = jnp.mean(values * values, axis=1, keepdims=True)
    normed = (values * lax.rsqrt(mean_square + 1e-06) * gain_ref[...]).astype(BF16)
    lane = lax.broadcasted_iota(jnp.int32, (ROWS, 128), 1)
    weights = jnp.zeros((ROWS, 128), F32)
    for k in range(8):
        held = jnp.sum(jnp.where(lane == pair_ref[:, k:k + 1], slot_ref[...], 0.0), axis=1, keepdims=True)
        weights = weights + jnp.where((lane & 63).astype(F32) == held, comb_ref[:, k:k + 1], 0.0)
    high = weights.astype(BF16)
    low = (weights - high.astype(F32)).astype(BF16)
    xa[z, y] = normed[:, :HALF]
    xb[y, z, :, :HALF] = normed[:, HALF:]
    xb[y, z, :, HALF:] = jnp.where(lane < 64, high.astype(F32), low.astype(F32)).astype(BF16)

    pl.semaphore_wait(barrier, NZ * NY + 2)

    def first_a(dy):
        return move(xa.at[z, y], xa.at[z, y], sem_s1.at[0], sem_a1, at(z, mod(y + dy, NY)))

    def first_b(dz):
        return move(xb.at[y, z], xb.at[y, z], sem_s1.at[1], sem_b1, at(mod(z + dz, NZ), y))

    def start_first(i, _):
        first_a(i).start()
        first_b(i).start()
        return 0

    lax.fori_loop(1, 8, start_first, 0)

    def offset(g):
        half = (g + 1) // 2
        odd = lax.rem(g, 2)
        return odd * half + (1 - odd) * lax.rem(NZ - half, NZ)

    own_w = pltpu.make_async_copy(w_ref.at[z * NY + y], wraw.at[core, x, z, y], w_own)
    own_w.start()

    def send_w(i, _):
        g, dy = i // NY, lax.rem(i, NY)
        zz, yy = mod(z + offset(g), NZ), mod(y + dy, NY)
        move(w_ref.at[zz * NY + yy], wraw.at[core, x, z, y], w_send, w_recv.at[g], at(zz, yy)).start()
        return 0

    lax.fori_loop(1, NZ * NY, send_w, 0)

    def block(half, index, part=None):
        ref = (xa, xb)[half]
        return ref.at[index] if part is None else ref.at[index, pl.ds(4 * part, 4)]

    def ring(half, way, step, part=None):
        sign = 1 - 2 * way
        mine = (z, y)[half]
        device = at(mod(z + sign, NZ), y) if half == 0 else at(z, mod(y + sign, NY))
        ref = block(half, mod(mine - sign * step, 8), part)
        index = (half * 2 + way) * 4 + step
        return move(ref, ref, ring_s.at[index], ring_r.at[index], device)

    def ring_landed(half, way, step, part=None):
        sign = 1 - 2 * way
        mine = (z, y)[half]
        ref = block(half, mod(mine - sign * (step + 1), 8), part)
        index = (half * 2 + way) * 4 + step
        move(ref, ref, ring_s.at[index], ring_r.at[index], right).wait_recv()

    def rows_step(step):
        if step == 0:
            move(xa.at[z, pl.ds(0, 7)], xa.at[z, pl.ds(0, 7)], sem_s1.at[0], sem_a1, right).wait_recv()
            move(xb.at[y, pl.ds(0, 7)], xb.at[y, pl.ds(0, 7)], sem_s1.at[1], sem_b1, right).wait_recv()
        for half in range(2):
            for way in range(2):
                if step > 0:
                    ring_landed(half, way, step - 1)
                ring(half, way, step, None if step < 3 else way).start()

    def rows_end():
        for half in range(2):
            for way in range(2):
                ring_landed(half, way, 3, way)
        mine = lax.broadcasted_iota(jnp.int32, (128, 128), 1) & 63
        mine = mine == z * NY + y

        def fill(i, _):
            for half in range(2):
                raw = xb[:, i, :, HALF:] if half == 0 else xb[i, :, :, HALF:]
                c = jnp.where(mine, raw.reshape(128, 128).astype(F32), 0.0)
                coef[half, i] = jnp.broadcast_to(jnp.sum(c, axis=1, keepdims=True), (128, 128))
            return 0

        lax.fori_loop(0, 8, fill, 0)

    acc[...] = jnp.zeros_like(acc)

    def multiply(g, _):
        zz = mod(z - offset(g), NZ)

        def tile(yy, _):
            for c in range(2):
                row = pl.multiple_of(yy * 32 + c * 16, 16)
                for t in range(TILES):
                    wmat[zz, pl.ds(row, 16), t * 128:(t + 1) * 128] = jnp.concatenate(
                        [wraw[c, i, zz, yy, t] for i in range(NX)], axis=0)
            return 0

        lax.fori_loop(0, NY, tile, 0)

        def add(rows_of, first):
            column = pl.multiple_of((zz - first) * 256, 256)

            def part(q, _):
                rows = rows_of(q, column)
                for n in range(3):
                    at_n = slice(n * 512, (n + 1) * 512)
                    spot = pl.ds(pl.multiple_of(q * 512, 512), 512)
                    acc[spot, at_n] += jnp.dot(rows, wmat[zz, :, at_n], preferred_element_type=F32)
                return 0

            lax.fori_loop(0, 2, part, 0)

        @pl.when(zz < 4)
        def _():
            add(lambda q, col: xa[pl.ds(q * 4, 4), :, :, pl.ds(col, 256)].reshape(512, 256), 0)

        @pl.when(zz >= 4)
        def _():
            add(lambda q, col: jnp.concatenate(
                [xb[:, q * 4 + i, :, pl.ds(col, 256)].reshape(128, 256) for i in range(4)], axis=0), 4)

        return 0

    def x_copy(g, way):
        zz = mod(z - offset(g), NZ)
        ref = wraw.at[core, x, zz]
        return move(ref, ref, x_send.at[way, g], x_recv.at[way, g], (right, left)[way])

    def x_forward(g, way):
        zz = mod(z - offset(g), NZ)
        ref = wraw.at[core, mod(x - 1 + 2 * way, NX), zz, pl.ds(4 * way, 4)]
        return move(ref, ref, f_send.at[way, g], f_recv.at[way, g], (right, left)[way])

    def core_copy(g):
        zz = mod(z - offset(g), NZ)
        ref = wraw.at[core, :, zz]
        return move(ref, ref, c_send.at[g], c_recv.at[g], other)

    def w_step(s, _):
        @pl.when(s < 8)
        def _():
            @pl.when(s == 0)
            def _():
                ref = wraw.at[core, x, z, pl.ds(0, 7)]
                move(ref, ref, w_send, w_recv.at[0], right).wait_recv()
                own_w.wait()

            @pl.when(s > 0)
            def _():
                ref = wraw.at[core, x, mod(z - offset(s), NZ)]
                move(ref, ref, w_send, w_recv.at[s], right).wait_recv()

            for way in range(2):
                x_copy(s, way).start()

        for i in range(4):
            pl.when(s == i)(lambda i=i: rows_step(i))
        pl.when(s == 4)(rows_end)

        @pl.when((s >= 1) & (s < 9))
        def _():
            for way in range(2):
                x_copy(s - 1, way).wait_recv()
                x_forward(s - 1, way).start()

        @pl.when((s >= 2) & (s < 10))
        def _():
            for way in range(2):
                x_forward(s - 2, way).wait_recv()
            core_copy(s - 2).start()

        @pl.when((s >= 3) & (s < 11))
        def _():
            core_copy(s - 3).wait_recv()

        @pl.when(s == 5)
        def _():
            lax.fori_loop(0, 3, multiply, 0)

        @pl.when(s > 5)
        def _():
            multiply(s - 3, 0)

        return 0

    lax.fori_loop(0, 11, w_step, 0)

    def activate(i, _):
        spot = pl.ds(pl.multiple_of(i * 128, 128), 128)
        gate, up = acc[spot, :F], acc[spot, F:]
        value = (gate / (1.0 + jnp.exp(-gate)) * up).astype(BF16).reshape(8, ROWS, F)
        hid[0, i] = value
        hid[1, :, i] = value
        return 0

    lax.fori_loop(0, 8, activate, 0)

    def term(half, index):
        rows = hid[half, index].reshape(128, F)
        scale = coef[half, index][:, :1]
        parts = [lax.dot_general(rows, wmat[half * 4 + i, :, 2 * F:], (((1,), (1,)), ((), ())),
                                 preferred_element_type=F32) for i in range(4)]
        return jnp.concatenate(parts, axis=1) * scale

    def beside(half, sign):
        return at(mod(z + (1 - half) * sign, NZ), mod(y + half * sign, NY))

    def mine_of(half):
        return (1 - half) * z + half * y

    def rs_first(half, way):
        ref = rs_send.at[half, way, 0, pl.ds(way * 64, 64)]
        dst = rs_recv.at[half, way, 0, pl.ds(way * 64, 64)]
        return move(ref, dst, rs_s.at[half, way, 0], rs_r.at[half, way, 0], beside(half, 1 - 2 * way))

    def rs_copy(half, way, step):
        return move(rs_send.at[half, way, step], rs_recv.at[half, way, step],
                    rs_s.at[half, way, step], rs_r.at[half, way, step], beside(half, 1 - 2 * way))

    def begin(half, _):
        value = term(half, mod(mine_of(half) + 4, 8)).astype(BF16)
        for way in range(2):
            rows = slice(way * 64, way * 64 + 64)
            rest = slice(64 - way * 64, 128 - way * 64)
            rs_send[half, way, 0, rows] = value[rows]
            rs_first(half, way).start()
            rs_recv[half, way, 0, rest] = jnp.zeros((64, HALF), BF16)
        return 0

    lax.fori_loop(0, 2, begin, 0)

    def go(i, _):
        step, half, way = 1 + i // 4, lax.rem(i // 2, 2), lax.rem(i, 2)
        sign = 1 - 2 * way
        value = term(half, mod(mine_of(half) + sign * (4 - step), 8))

        @pl.when(step == 1)
        def _():
            rs_first(half, way).wait_recv()

        @pl.when(step > 1)
        def _():
            rs_copy(half, way, step - 1).wait_recv()

        rs_send[half, way, step] = (value + rs_recv[half, way, step - 1].astype(F32)).astype(BF16)
        rs_copy(half, way, step).start()
        return 0

    def fin_copy(half, step):
        mine = (1 - half) * y + half * z
        there = mod(mine + step, 8)
        device = at((1 - half) * z + half * there, (1 - half) * there + half * y)
        return move(fin_send.at[half, there], fin_recv.at[half, mine], fin_s.at[half], fin_r.at[half], device)

    def end(half, _):
        value = term(half, mine_of(half))
        for way in range(2):
            rs_copy(half, way, 3).wait_recv()
            value = value + rs_recv[half, way, 3].astype(F32)
        value = value.astype(BF16).reshape(8, ROWS, HALF)
        fin_send[half] = value

        def spread(step, _):
            fin_copy(half, step).start()
            return 0

        lax.fori_loop(1, 8, spread, 0)
        mine = (1 - half) * y + half * z
        fin_recv[half, mine] = fin_send[half, mine]
        return 0

    lax.fori_loop(0, 12, go, 0)
    lax.fori_loop(0, 2, end, 0)

    for half in range(2):
        ref = fin_recv.at[half, pl.ds(0, 7)]
        move(ref, ref, fin_s.at[half], fin_r.at[half], right).wait_recv()
        total = fin_recv[half, 0].astype(F32)
        for i in range(1, 8):
            total = total + fin_recv[half, i].astype(F32)
        out_ref[:, half * HALF:(half + 1) * HALF] = total.astype(BF16)

    move(xa.at[z, pl.ds(0, 7)], xa.at[z, pl.ds(0, 7)], sem_s1.at[0], sem_a1, right).wait_send()
    move(xb.at[y, pl.ds(0, 7)], xb.at[y, pl.ds(0, 7)], sem_s1.at[1], sem_b1, right).wait_send()
    ref = w_ref.at[pl.ds(0, NZ * NY - 1)]
    move(ref, ref, w_send, w_recv.at[0], right).wait_send()
    for half in range(2):
        for way in range(2):
            for step in range(4):
                ring(half, way, step, None if step < 3 else way).wait_send()
            rs_first(half, way).wait_send()
            for step in range(1, 4):
                rs_copy(half, way, step).wait_send()
        ref = fin_send.at[half, pl.ds(0, 7)]
        move(ref, ref, fin_s.at[half], fin_r.at[half], right).wait_send()

    def drain(g, _):
        for way in range(2):
            x_copy(g, way).wait_send()
            x_forward(g, way).wait_send()
        core_copy(g).wait_send()
        return 0

    lax.fori_loop(0, 8, drain, 0)


def per_device(tokens, norm_gain, expert_weights, slot_expert, pair_slots, combine_weights):
    pieces = expert_weights.reshape(NZ * NY, NX, TILES, 128).transpose(0, 2, 1, 3)
    vmem = pl.BlockSpec(memory_space=pltpu.VMEM)
    sem = pltpu.SemaphoreType.DMA
    return pl.pallas_call(
        kernel,
        out_shape=jax.ShapeDtypeStruct((ROWS, D), BF16),
        in_specs=[vmem, vmem, pl.BlockSpec(memory_space=pl.ANY), vmem, vmem, vmem],
        out_specs=vmem,
        scratch_shapes=[
            pltpu.VMEM((8, 8, ROWS, HALF), BF16),
            pltpu.VMEM((8, 8, ROWS, HALF + 128), BF16),
            pltpu.VMEM((2, NX, NZ, NY, TILES, 4, 128), BF16),
            pltpu.VMEM((8, 256, 3 * F), BF16),
            pltpu.VMEM((1024, 2 * F), F32),
            pltpu.VMEM((2, 8, 8, ROWS, F), BF16),
            pltpu.VMEM((2, 8, 128, 128), F32),
            pltpu.VMEM((2, 2, 4, 128, HALF), BF16),
            pltpu.VMEM((2, 2, 4, 128, HALF), BF16),
            pltpu.VMEM((2, 8, ROWS, HALF), BF16),
            pltpu.VMEM((2, 8, ROWS, HALF), BF16),
            sem, sem, sem((2,)), sem((16,)), sem((16,)), sem((8,)), sem, sem,
            sem((2, 8)), sem((2, 8)), sem((2, 8)), sem((2, 8)), sem((8,)), sem((8,)),
            sem((2, 2, 4)), sem((2, 2, 4)), sem((2,)), sem((2,)),
        ],
        compiler_params=pltpu.CompilerParams(
            collective_id=0, has_side_effects=True, vmem_limit_bytes=56 * 2**20),
    )(tokens, norm_gain.reshape(1, D), pieces, slot_expert.astype(F32).reshape(1, 128), pair_slots, combine_weights)


def solution(mesh):
    placed = (
        P(("dp", "rep"), None),
        P(),
        P(None, ("dp", "rep"), None),
        P(),
        P(("dp", "rep"), None),
        P(("dp", "rep"), None),
    )
    return jax.shard_map(
        per_device, mesh=mesh, in_specs=placed, out_specs=P(("dp", "rep"), None), check_vma=False
    )
```

time: 463 us -> 161 us (0.35)
  waiting for transfers between devices: 329 us -> 0 us
  Pallas kernels: 0 us -> 154 us
  starting transfers between devices: 73.5 us -> 0 us
  local copies, waits for them, and re-layouts: 23.9 us -> 4.18 us
  between operations: 13.5 us -> 0.01 us
  other arithmetic: 10.6 us -> 1.18 us
  matrix products: 9.05 us -> 0 us
    all_to_all x3 -> x0, waiting for transfers between devices: 290 us -> none  [the longest x1 260 us: per_device(): lax.all_to_all(outgoing, 'dp', split_axis=0, concat_axis=0, tiled=True)]
    pallas_call x0 -> x1, Pallas kernels: none -> 154 us  [per_device(): pl.pallas_call(kernel, out_shape=jax.ShapeDtypeStruct((ROWS, D), BF16), i...]
    all_to_all x3 -> x0, starting transfers between devices: 73.5 us -> none  [the longest x1 40.3 us: per_device(): lax.all_to_all(result, 'dp', split_axis=0, concat_axis=0, tiled=True)]
    all_gather x1 -> x0, waiting for transfers between devices: 38.3 us -> none  [per_device(): blocks = lax.all_gather(expert_weights, 'rep', axis=1, tiled=True)]
    gather x1 -> x0, local copies, waits for them, and re-layouts: 9.57 us -> none  [per_device(): outgoing = jnp.take(blocks, slot_expert, axis=0)]
    dot_general x4 -> x0, matrix products: 9.05 us -> none  [the longest x1 4.56 us: per_device(): jnp.dot(rows, weight[:, :2 * hidden_units], preferred_element_type=jnp.fl...]
    select_n x2 -> x0, other arithmetic: 8.24 us -> none  [per_device(): outgoing = jnp.take(blocks, slot_expert, axis=0)]
    all_gather x1 -> x0, local copies, waits for them, and re-layouts: 7.09 us -> none  [per_device(): blocks = lax.all_gather(expert_weights, 'rep', axis=1, tiled=True)]
  transfers between devices with their start and end apart: 4 -> 0, of which waited for: 3 -> 0; matrix products, arithmetic and copies ran while one was open for 7% -> 0% of each run, Pallas kernels for 0% -> 0%
where the time goes in v1:
time: 161 us; the launch traced here: 159 us
  Pallas kernels  154 us (96%)
  local copies, waits for them, and re-layouts  4.18 us (3%)
    pallas_call x1, Pallas kernels, per_device(): pl.pallas_call(kernel, out_shape=jax.ShapeDtypeStruct((ROWS, D), BF16), i...  154 us
    unnamed x3, local copies, waits for them, and re-layouts  4.18 us

profile of v1, /device:TPU:6, one launch (start us, length us, event | category | flops | bytes accessed | tf_op | source)
XLA Modules:
  0.0 159.0 jit_solution(13692156244312110310)
XLA Ops:
  0.0 1.2 convert_bitcast_fusion.slot_ref
  1.2 1.4 copy.7.pair_ref
  2.5 1.3 copy.8.comb_ref
  3.9 153.6 %shard_map.64 = bf16[16,2048]{1,0:T(8,128)(2,1)} custom-call(bf16[16,2048]{1,0:T(8,128)(2,1)} %tok_ref.1, f32[1,2048]{1,0:T(1,128)} %bitcast.7, bf16[64,18,4,128]{3,2,1,0:T(4,128)(2,1)} %bitcast.6, f32[1,128]{1,0:T(1,128)} %convert_bitcast_fusion.slot_ref, s32[16,8]{1,0:T(8,128)} %copy.7.pair_ref, f32[16,8]{1,0:T(8,128)} %copy.8.comb_ref), custom_call_target="tpu_custom_call" | custom-call | tf_op jit(solution)/shard_map/pallas_call | solution.py:365
  157.5 1.5 copy.10

commit v2 on v1

v2 whole, which is shorter than its diff:
```python
import jax
import jax.numpy as jnp
from jax import lax
from jax.experimental import pallas as pl
from jax.experimental.pallas import tpu as pltpu
from jax.sharding import PartitionSpec as P

NZ, NY, NX = 8, 8, 4
D, F, ROWS = 2048, 768, 16
HALF = D // 2
TILES = 3 * F // 128
BF16, F32 = jnp.bfloat16, jnp.float32


def mod(value, size):
    return lax.rem(value + 2 * size, size)


def kernel(tok_ref, gain_ref, w_ref, slot_ref, pair_ref, comb_ref, out_ref,
           xa, xb, wz, wraw, wmat, acc, hid, coef, terms, rs_send, rs_recv, fin_send, fin_recv,
           sem_a1, sem_b1, sem_s1, ring_r, ring_s, z_recv, z_send, y_recv, y_send, w_own,
           x_recv, x_send, f_recv, f_send, c_recv, c_send,
           rs_r, rs_s, fin_r, fin_s):
    dp, x = lax.axis_index("dp"), lax.axis_index("rep")
    z, y, core = dp // (2 * NY), lax.rem(dp // 2, NY), lax.rem(dp, 2)

    def at(zz, yy):
        return (zz * (2 * NY) + yy * 2 + core, x)

    def move(src, dst, send, recv, device):
        return pltpu.make_async_remote_copy(
            src_ref=src, dst_ref=dst, send_sem=send, recv_sem=recv,
            device_id=device, device_id_type=pl.DeviceIdType.MESH)

    right, left = (dp, mod(x + 1, NX)), (dp, mod(x - 1, NX))
    other = (dp + 1 - 2 * core, x)

    barrier = pltpu.get_barrier_semaphore()

    def greet(i, _):
        for device in (at(mod(z + i, NZ), y), at(z, mod(y + i, NY))):
            pl.semaphore_signal(barrier, inc=1, device_id=device, device_id_type=pl.DeviceIdType.MESH)
        return 0

    lax.fori_loop(1, 8, greet, 0)
    for device in (right, left, other):
        pl.semaphore_signal(barrier, inc=1, device_id=device, device_id_type=pl.DeviceIdType.MESH)

    values = tok_ref[...].astype(F32)
    mean_square = jnp.mean(values * values, axis=1, keepdims=True)
    normed = (values * lax.rsqrt(mean_square + 1e-06) * gain_ref[...]).astype(BF16)
    lane = lax.broadcasted_iota(jnp.int32, (ROWS, 128), 1)
    weights = jnp.zeros((ROWS, 128), F32)
    slots, pairs, combs = slot_ref[...].astype(F32), pair_ref[...].T, comb_ref[...].T
    for k in range(8):
        held = jnp.sum(jnp.where(lane == pairs[:, k:k + 1], slots, 0.0), axis=1, keepdims=True)
        weights = weights + jnp.where((lane & 63).astype(F32) == held, combs[:, k:k + 1], 0.0)
    high = weights.astype(BF16)
    low = (weights - high.astype(F32)).astype(BF16)
    xa[z, y] = normed[:, :HALF]
    xb[y, z, :, :HALF] = normed[:, HALF:]
    xb[y, z, :, HALF:] = jnp.where(lane < 64, high.astype(F32), low.astype(F32)).astype(BF16)

    acc[...] = jnp.zeros_like(acc)
    pl.semaphore_wait(barrier, 17)

    def offset(g):
        half = (g + 1) // 2
        odd = lax.rem(g, 2)
        return odd * half + (1 - odd) * lax.rem(NZ - half, NZ)

    def z_copy(g):
        zz = mod(z + offset(g), NZ)
        return move(w_ref.at[pl.ds(zz * NY, NY)], wz.at[z], z_send.at[g], z_recv.at[g], at(zz, y))

    def y_spread(g, source):
        zz = mod(z - offset(g), NZ)

        def one(i, _):
            yy = mod(y + offset(i), NY)
            move(source(zz, yy), wraw.at[core, x, zz, y], y_send.at[g], y_recv.at[g], at(z, yy)).start()
            return 0

        lax.fori_loop(1, NY, one, 0)
        pltpu.make_async_copy(source(zz, y), wraw.at[core, x, zz, y], w_own.at[g]).start()

    def y_landed(g):
        zz = mod(z - offset(g), NZ)
        ref = wraw.at[core, x, zz, pl.ds(0, 7)]
        move(ref, ref, y_send.at[g], y_recv.at[g], right).wait_recv()
        ref = wraw.at[core, x, zz, y]
        pltpu.make_async_copy(ref, ref, w_own.at[g]).wait()

    z_copy(1).start()
    z_copy(2).start()
    y_spread(0, lambda zz, yy: w_ref.at[zz * NY + yy])

    def first_a(dy):
        return move(xa.at[z, y], xa.at[z, y], sem_s1.at[0], sem_a1, at(z, mod(y + dy, NY)))

    def first_b(dz):
        return move(xb.at[y, z], xb.at[y, z], sem_s1.at[1], sem_b1, at(mod(z + dz, NZ), y))

    def start_first(i, _):
        first_a(offset(i)).start()
        first_b(offset(i)).start()
        return 0

    lax.fori_loop(1, 8, start_first, 0)

    def ring(half, way, step, part, ahead=0):
        sign = 1 - 2 * way
        mine = (z, y)[half]
        device = at(mod(z + sign, NZ), y) if half == 0 else at(z, mod(y + sign, NY))
        ref = (xa, xb)[half].at[mod(mine - sign * (step + ahead), 8), pl.ds(2 * part, 2)]
        index = ((half * 2 + way) * 4 + step) * 4 + part
        return move(ref, ref, ring_s.at[index], ring_r.at[index], device)

    def ring_landed(half, way, step, part):
        ring(half, way, step, part, 1).wait_recv()

    def rows_first():
        move(xa.at[z, pl.ds(0, 7)], xa.at[z, pl.ds(0, 7)], sem_s1.at[0], sem_a1, right).wait_recv()
        move(xb.at[y, pl.ds(0, 7)], xb.at[y, pl.ds(0, 7)], sem_s1.at[1], sem_b1, right).wait_recv()

    def rows_step(j, _):
        step = j // 4
        for half in range(2):
            for way in range(2):
                part = lax.rem(j, 4) + 2 * way * (step // 3)

                @pl.when(step > 0)
                def _(half=half, way=way, part=part):
                    ring_landed(half, way, step - 1, part)

                ring(half, way, step, part).start()
        return 0

    def rows_end():
        for half in range(2):
            for way in range(2):
                for i in range(2):
                    ring_landed(half, way, 2, 2 * (1 - way) + i)
                    ring_landed(half, way, 3, 2 * way + i)
        mine = lax.broadcasted_iota(jnp.int32, (128, 128), 1) & 63
        mine = mine == z * NY + y

        def fill(i, _):
            for half in range(2):
                raw = xb[:, i, :, HALF:] if half == 0 else xb[i, :, :, HALF:]
                c = jnp.where(mine, raw.reshape(128, 128).astype(F32), 0.0)
                coef[half, i] = jnp.broadcast_to(jnp.sum(c, axis=1, keepdims=True), (128, 128))
            return 0

        lax.fori_loop(0, 8, fill, 0)

    def multiply(g, _):
        zz = mod(z - offset(g), NZ)

        def tile(yy, _):
            for c in range(2):
                row = pl.multiple_of(yy * 32 + c * 16, 16)
                for t in range(TILES):
                    wmat[zz, pl.ds(row, 16), t * 128:(t + 1) * 128] = jnp.concatenate(
                        [wraw[c, i, zz, yy, t] for i in range(NX)], axis=0)
            return 0

        lax.fori_loop(0, NY, tile, 0)

        def add(rows_of, first):
            column = pl.multiple_of((zz - first) * 256, 256)

            def part(q, _):
                rows = rows_of(q, column)
                for n in range(3):
                    at_n = slice(n * 512, (n + 1) * 512)
                    spot = pl.ds(pl.multiple_of(q * 512, 512), 512)
                    acc[spot, at_n] += jnp.dot(rows, wmat[zz, :, at_n], preferred_element_type=F32)
                return 0

            lax.fori_loop(0, 2, part, 0)

        @pl.when(zz < 4)
        def _():
            add(lambda q, col: xa[pl.ds(q * 4, 4), :, :, pl.ds(col, 256)].reshape(512, 256), 0)

        @pl.when(zz >= 4)
        def _():
            add(lambda q, col: jnp.concatenate(
                [xb[:, q * 4 + i, :, pl.ds(col, 256)].reshape(128, 256) for i in range(4)], axis=0), 4)

        return 0

    def x_copy(g, way):
        zz = mod(z - offset(g), NZ)
        ref = wraw.at[core, x, zz]
        return move(ref, ref, x_send.at[way, g], x_recv.at[way, g], (right, left)[way])

    def x_forward(g, way):
        zz = mod(z - offset(g), NZ)
        ref = wraw.at[core, mod(x - 1 + 2 * way, NX), zz, pl.ds(4 * way, 4)]
        return move(ref, ref, f_send.at[way, g], f_recv.at[way, g], (right, left)[way])

    def core_copy(g):
        zz = mod(z - offset(g), NZ)
        ref = wraw.at[core, :, zz]
        return move(ref, ref, c_send.at[g], c_recv.at[g], other)

    def w_step(s, _):
        @pl.when(s < 5)
        def _():
            z_copy(s + 3).start()

        @pl.when(s < 7)
        def _():
            z_copy(s + 1).wait_recv()
            y_spread(s + 1, lambda zz, yy: wz.at[zz, yy])

        @pl.when(s < 8)
        def _():
            y_landed(s)
            for way in range(2):
                x_copy(s, way).start()

        pl.when(s == 0)(rows_first)

        @pl.when(s < 5)
        def _():
            lax.fori_loop(3 * s, jnp.minimum(3 * s + 3, 14), rows_step, 0)

        pl.when(s == 5)(rows_end)

        @pl.when((s >= 1) & (s < 9))
        def _():
            for way in range(2):
                x_copy(s - 1, way).wait_recv()
                x_forward(s - 1, way).start()

        @pl.when((s >= 2) & (s < 10))
        def _():
            for way in range(2):
                x_forward(s - 2, way).wait_recv()
            core_copy(s - 2).start()

        @pl.when((s >= 3) & (s < 11))
        def _():
            core_copy(s - 3).wait_recv()

        @pl.when(s == 5)
        def _():
            lax.fori_loop(0, 3, multiply, 0)

        @pl.when(s > 5)
        def _():
            multiply(s - 3, 0)

        return 0

    lax.fori_loop(0, 11, w_step, 0)

    def activate(i, _):
        spot = pl.ds(pl.multiple_of(i * 128, 128), 128)
        gate, up = acc[spot, :F], acc[spot, F:]
        value = (gate / (1.0 + jnp.exp(-gate)) * up).astype(BF16).reshape(8, ROWS, F)
        hid[0, i] = value
        hid[1, :, i] = value
        return 0

    lax.fori_loop(0, 8, activate, 0)

    def term(half, index):
        rows = hid[half, index].reshape(128, F)
        scale = coef[half, index][:, :1]
        parts = [lax.dot_general(rows, wmat[half * 4 + i, :, 2 * F:], (((1,), (1,)), ((), ())),
                                 preferred_element_type=F32) for i in range(4)]
        return jnp.concatenate(parts, axis=1) * scale

    def beside(half, sign):
        return at(mod(z + (1 - half) * sign, NZ), mod(y + half * sign, NY))

    def mine_of(half):
        return (1 - half) * z + half * y

    def rs_rows(way, part):
        start = 64 * way if part else 64 - 64 * way
        return slice(start, start + 64)

    def rs_copy(half, way, step, part):
        rows = pl.ds(rs_rows(way, part).start, 64)
        return move(rs_send.at[half, way, step, rows], rs_recv.at[half, way, step, rows],
                    rs_s.at[half, way, step, part], rs_r.at[half, way, step, part], beside(half, 1 - 2 * way))

    def begin(half, _):
        value = term(half, mod(mine_of(half) + 4, 8)).astype(BF16)
        for way in range(2):
            rs_send[half, way, 0, rs_rows(way, 1)] = value[rs_rows(way, 1)]
            rs_copy(half, way, 0, 1).start()
        return 0

    lax.fori_loop(0, 2, begin, 0)

    def go(step, _):
        def prepare(half, _):
            for way in range(2):
                terms[half, way] = term(half, mod(mine_of(half) + (1 - 2 * way) * (4 - step), 8))
            return 0

        lax.fori_loop(0, 2, prepare, 0)

        def pass_on(half, part, way, first):
            rows = rs_rows(way, part)
            value = terms[half, way, rows]
            if not first:
                rs_copy(half, way, step - 1, part).wait_recv()
                value = value + rs_recv[half, way, step - 1, rows].astype(F32)
            rs_send[half, way, step, rows] = value.astype(BF16)
            rs_copy(half, way, step, part).start()

        for part in range(2):
            def each(half, _):
                for way in range(2):
                    if part == 0:
                        pl.when(step == 1)(lambda: pass_on(half, part, way, True))
                        pl.when(step > 1)(lambda: pass_on(half, part, way, False))
                    else:
                        pass_on(half, part, way, False)
                return 0

            lax.fori_loop(0, 2, each, 0)
        return 0

    def fin_spread(half, there):
        mine = (1 - half) * y + half * z
        device = at((1 - half) * z + half * there, (1 - half) * there + half * y)

        @pl.when(there != mine)
        def _():
            move(fin_send.at[half, there], fin_recv.at[half, mine], fin_s.at[half], fin_r.at[half], device).start()

    def end(half, _):
        terms[half, 0] = term(half, mine_of(half))
        for part in range(2):
            rows = slice(64 * part, 64 * part + 64)
            value = terms[half, 0, rows]
            for way in range(2):
                rs_copy(half, way, 3, int(part == way)).wait_recv()
                value = value + rs_recv[half, way, 3, rows].astype(F32)
            fin_send[half, 4 * part:4 * part + 4] = value.astype(BF16).reshape(4, ROWS, HALF)
            for i in range(4):
                fin_spread(half, 4 * part + i)
        mine = (1 - half) * y + half * z
        fin_recv[half, mine] = fin_send[half, mine]
        return 0

    lax.fori_loop(1, 4, go, 0)
    lax.fori_loop(0, 2, end, 0)

    for half in range(2):
        ref = fin_recv.at[half, pl.ds(0, 7)]
        move(ref, ref, fin_s.at[half], fin_r.at[half], right).wait_recv()
        total = fin_recv[half, 0].astype(F32)
        for i in range(1, 8):
            total = total + fin_recv[half, i].astype(F32)
        out_ref[:, half * HALF:(half + 1) * HALF] = total.astype(BF16)

    move(xa.at[z, pl.ds(0, 7)], xa.at[z, pl.ds(0, 7)], sem_s1.at[0], sem_a1, right).wait_send()
    move(xb.at[y, pl.ds(0, 7)], xb.at[y, pl.ds(0, 7)], sem_s1.at[1], sem_b1, right).wait_send()
    for half in range(2):
        for way in range(2):
            rs_copy(half, way, 0, 1).wait_send()
            for step in range(1, 4):
                for part in range(2):
                    rs_copy(half, way, step, part).wait_send()
        ref = fin_send.at[half, pl.ds(0, 7)]
        move(ref, ref, fin_s.at[half], fin_r.at[half], right).wait_send()

    def ring_drain(j, _):
        step = j // 4
        for half in range(2):
            for way in range(2):
                ring(half, way, step, lax.rem(j, 4) + 2 * way * (step // 3)).wait_send()
        return 0

    lax.fori_loop(0, 14, ring_drain, 0)

    def drain(g, _):
        for way in range(2):
            x_copy(g, way).wait_send()
            x_forward(g, way).wait_send()
        core_copy(g).wait_send()
        ref = wz.at[0, pl.ds(0, 7)]
        move(ref, ref, y_send.at[g], y_recv.at[g], right).wait_send()

        @pl.when(g > 0)
        def _():
            z_copy(g).wait_send()

        return 0

    lax.fori_loop(0, 8, drain, 0)


def per_device(tokens, norm_gain, expert_weights, slot_expert, pair_slots, combine_weights):
    pieces = expert_weights.reshape(NZ * NY, NX, TILES, 128).transpose(0, 2, 1, 3)
    vmem = pl.BlockSpec(memory_space=pltpu.VMEM)
    sem = pltpu.SemaphoreType.DMA
    return pl.pallas_call(
        kernel,
        out_shape=jax.ShapeDtypeStruct((ROWS, D), BF16),
        in_specs=[vmem, vmem, pl.BlockSpec(memory_space=pl.ANY), vmem, vmem, vmem],
        out_specs=vmem,
        scratch_shapes=[
            pltpu.VMEM((8, 8, ROWS, HALF), BF16),
            pltpu.VMEM((8, 8, ROWS, HALF + 128), BF16),
            pltpu.VMEM((NZ, NY, TILES, 4, 128), BF16),
            pltpu.VMEM((2, NX, NZ, NY, TILES, 4, 128), BF16),
            pltpu.VMEM((8, 256, 3 * F), BF16),
            pltpu.VMEM((1024, 2 * F), F32),
            pltpu.VMEM((2, 8, 8, ROWS, F), BF16),
            pltpu.VMEM((2, 8, 128, 128), F32),
            pltpu.VMEM((2, 2, 128, HALF), F32),
            pltpu.VMEM((2, 2, 4, 128, HALF), BF16),
            pltpu.VMEM((2, 2, 4, 128, HALF), BF16),
            pltpu.VMEM((2, 8, ROWS, HALF), BF16),
            pltpu.VMEM((2, 8, ROWS, HALF), BF16),
            sem, sem, sem((2,)), sem((64,)), sem((64,)), sem((8,)), sem((8,)), sem((8,)), sem((8,)), sem((8,)),
            sem((2, 8)), sem((2, 8)), sem((2, 8)), sem((2, 8)), sem((8,)), sem((8,)),
            sem((2, 2, 4, 2)), sem((2, 2, 4, 2)), sem((2,)), sem((2,)),
        ],
        compiler_params=pltpu.CompilerParams(
            collective_id=0, has_side_effects=True, vmem_limit_bytes=56 * 2**20),
    )(tokens, norm_gain.reshape(1, D), pieces, slot_expert.reshape(1, 128), pair_slots.T, combine_weights.T)


def solution(mesh):
    placed = (
        P(("dp", "rep"), None),
        P(),
        P(None, ("dp", "rep"), None),
        P(),
        P(("dp", "rep"), None),
        P(("dp", "rep"), None),
    )
    return jax.shard_map(
        per_device, mesh=mesh, in_specs=placed, out_specs=P(("dp", "rep"), None), check_vma=False
    )
```

time: 161 us -> 133 us (0.83); the launches traced: 159 us -> 133 us
  Pallas kernels: 154 us -> 131 us
  local copies, waits for them, and re-layouts: 4.18 us -> 1.47 us
    pallas_call x1, Pallas kernels: 154 us -> 131 us  [per_device(): pl.pallas_call(kernel, out_shape=jax.ShapeDtypeStruct((ROWS, D), BF16), i...]
    unnamed x3 -> x1, local copies, waits for them, and re-layouts: 4.18 us -> 1.47 us
where the time goes in v2:
time: 133 us
  Pallas kernels  131 us (98%)
  local copies, waits for them, and re-layouts  1.47 us (1%)
    pallas_call x1, Pallas kernels, per_device(): pl.pallas_call(kernel, out_shape=jax.ShapeDtypeStruct((ROWS, D), BF16), i...  131 us

profile of v2, /device:TPU:6, one launch (start us, length us, event | category | flops | bytes accessed | tf_op | source)
XLA Modules:
  0.0 132.6 jit_solution(8268553957752075359)
XLA Ops:
  0.0 131.2 %shard_map.64 = bf16[16,2048]{1,0:T(8,128)(2,1)} custom-call(bf16[16,2048]{1,0:T(8,128)(2,1)} %tok_ref.1, f32[1,2048]{1,0:T(1,128)} %bitcast.8, bf16[64,18,4,128]{3,2,1,0:T(4,128)(2,1)} %bitcast.7, s32[1,128]{1,0:T(1,128)} %bitcast.11, s32[8,16]{1,0:T(8,128)} %bitcast.9, f32[8,16]{1,0:T(8,128)} %bitcast.10), custom_call_target="tpu_custom_call" | custom-call | tf_op jit(solution)/shard_map/pallas_call | solution.py:407
  131.2 1.5 %copy.8 = bf16[16,2048]{1,0:T(8,128)(2,1)} copy(bf16[16,2048]{1,0:T(8,128)(2,1)} %shard_map.64) | data formatting | bytes 131072

commit v3 on v2

--- a/solution.py
+++ b/solution.py
@@ -10,6 +10,7 @@
 HALF = D // 2
 TILES = 3 * F // 128
 BF16, F32 = jnp.bfloat16, jnp.float32
+FIRST, RING, READY, SLOTS = 0, 4, 9, 3
 
 
 def mod(value, size):
@@ -18,7 +19,7 @@
 
 def kernel(tok_ref, gain_ref, w_ref, slot_ref, pair_ref, comb_ref, out_ref,
            xa, xb, wz, wraw, wmat, acc, hid, coef, terms, rs_send, rs_recv, fin_send, fin_recv,
-           sem_a1, sem_b1, sem_s1, ring_r, ring_s, z_recv, z_send, y_recv, y_send, w_own,
+           first_r, first_s, ring_r, ring_s, z_recv, z_send, y_recv, y_send, w_own,
            x_recv, x_send, f_recv, f_send, c_recv, c_send,
            rs_r, rs_s, fin_r, fin_s):
     dp, x = lax.axis_index("dp"), lax.axis_index("rep")
@@ -45,6 +46,40 @@
     lax.fori_loop(1, 8, greet, 0)
     for device in (right, left, other):
         pl.semaphore_signal(barrier, inc=1, device_id=device, device_id_type=pl.DeviceIdType.MESH)
+
+    acc[...] = jnp.zeros_like(acc)
+    pl.semaphore_wait(barrier, 17)
+
+    def offset(g):
+        half = (g + 1) // 2
+        odd = lax.rem(g, 2)
+        return odd * half + (1 - odd) * lax.rem(NZ - half, NZ)
+
+    def z_copy(g):
+        zz = mod(z + offset(g), NZ)
+        return move(w_ref.at[pl.ds(zz * NY, NY)], wz.at[z], z_send.at[g], z_recv.at[g], at(zz, y))
+
+    def y_spread(g, source):
+        zz = mod(z - offset(g), NZ)
+
+        def one(i, _):
+            yy = mod(y + offset(i), NY)
+            move(source(zz, yy), wraw.at[core, x, zz, y], y_send.at[g], y_recv.at[g], at(z, yy)).start()
+            return 0
+
+        lax.fori_loop(1, NY, one, 0)
+        pltpu.make_async_copy(source(zz, y), wraw.at[core, x, zz, y], w_own.at[g]).start()
+
+    def y_landed(g):
+        zz = mod(z - offset(g), NZ)
+        ref = wraw.at[core, x, zz, pl.ds(0, 7)]
+        move(ref, ref, y_send.at[g], y_recv.at[g], right).wait_recv()
+        ref = wraw.at[core, x, zz, y]
+        pltpu.make_async_copy(ref, ref, w_own.at[g]).wait()
+
+    y_spread(0, lambda zz, yy: w_ref.at[zz * NY + yy])
+    for g in range(1, 5):
+        z_copy(g).start()
 
     values = tok_ref[...].astype(F32)
     mean_square = jnp.mean(values * values, axis=1, keepdims=True)
@@ -61,52 +96,21 @@
     xb[y, z, :, :HALF] = normed[:, HALF:]
     xb[y, z, :, HALF:] = jnp.where(lane < 64, high.astype(F32), low.astype(F32)).astype(BF16)
 
-    acc[...] = jnp.zeros_like(acc)
-    pl.semaphore_wait(barrier, 17)
-
-    def offset(g):
-        half = (g + 1) // 2
-        odd = lax.rem(g, 2)
-        return odd * half + (1 - odd) * lax.rem(NZ - half, NZ)
-
-    def z_copy(g):
-        zz = mod(z + offset(g), NZ)
-        return move(w_ref.at[pl.ds(zz * NY, NY)], wz.at[z], z_send.at[g], z_recv.at[g], at(zz, y))
-
-    def y_spread(g, source):
-        zz = mod(z - offset(g), NZ)
-
-        def one(i, _):
-            yy = mod(y + offset(i), NY)
-            move(source(zz, yy), wraw.at[core, x, zz, y], y_send.at[g], y_recv.at[g], at(z, yy)).start()
-            return 0
-
-        lax.fori_loop(1, NY, one, 0)
-        pltpu.make_async_copy(source(zz, y), wraw.at[core, x, zz, y], w_own.at[g]).start()
-
-    def y_landed(g):
-        zz = mod(z - offset(g), NZ)
-        ref = wraw.at[core, x, zz, pl.ds(0, 7)]
-        move(ref, ref, y_send.at[g], y_recv.at[g], right).wait_recv()
-        ref = wraw.at[core, x, zz, y]
-        pltpu.make_async_copy(ref, ref, w_own.at[g]).wait()
-
-    z_copy(1).start()
-    z_copy(2).start()
-    y_spread(0, lambda zz, yy: w_ref.at[zz * NY + yy])
-
-    def first_a(dy):
-        return move(xa.at[z, y], xa.at[z, y], sem_s1.at[0], sem_a1, at(z, mod(y + dy, NY)))
-
-    def first_b(dz):
-        return move(xb.at[y, z], xb.at[y, z], sem_s1.at[1], sem_b1, at(mod(z + dz, NZ), y))
-
-    def start_first(i, _):
-        first_a(offset(i)).start()
-        first_b(offset(i)).start()
-        return 0
-
-    lax.fori_loop(1, 8, start_first, 0)
+    def first(half, way, step, ahead=0):
+        sign = 1 - 2 * way
+        mine = (y, z)[half]
+        device = at(z, mod(y + sign, NY)) if half == 0 else at(mod(z + sign, NZ), y)
+        ref = (xa.at[z], xb.at[y])[half].at[mod(mine - sign * (step + ahead), 8)]
+        index = (half * 2 + way) * 4 + step
+        return move(ref, ref, first_s.at[index], first_r.at[index], device)
+
+    def first_step(step):
+        for half in range(2):
+            for way in range(2):
+                if step > 0 and (way == half or step < 4):
+                    first(half, way, step - 1, 1).wait_recv()
+                if step < 3 + (way == half):
+                    first(half, way, step).start()
 
     def ring(half, way, step, part, ahead=0):
         sign = 1 - 2 * way
@@ -119,10 +123,6 @@
     def ring_landed(half, way, step, part):
         ring(half, way, step, part, 1).wait_recv()
 
-    def rows_first():
-        move(xa.at[z, pl.ds(0, 7)], xa.at[z, pl.ds(0, 7)], sem_s1.at[0], sem_a1, right).wait_recv()
-        move(xb.at[y, pl.ds(0, 7)], xb.at[y, pl.ds(0, 7)], sem_s1.at[1], sem_b1, right).wait_recv()
-
     def rows_step(j, _):
         step = j // 4
         for half in range(2):
@@ -154,7 +154,7 @@
 
         lax.fori_loop(0, 8, fill, 0)
 
-    def multiply(g, _):
+    def place(g):
         zz = mod(z - offset(g), NZ)
 
         def tile(yy, _):
@@ -167,6 +167,9 @@
 
         lax.fori_loop(0, NY, tile, 0)
 
+    def multiply(g, _):
+        zz = mod(z - offset(g), NZ)
+
         def add(rows_of, first):
             column = pl.multiple_of((zz - first) * 256, 256)
 
@@ -174,8 +177,8 @@
                 rows = rows_of(q, column)
                 for n in range(3):
                     at_n = slice(n * 512, (n + 1) * 512)
-                    spot = pl.ds(pl.multiple_of(q * 512, 512), 512)
-                    acc[spot, at_n] += jnp.dot(rows, wmat[zz, :, at_n], preferred_element_type=F32)
+                    part_of = jnp.dot(rows, wmat[zz, :, at_n], preferred_element_type=F32)
+                    acc[pl.ds(q * 4, 4), :, :, at_n] += part_of.reshape(4, 8, ROWS, 512)
                 return 0
 
             lax.fori_loop(0, 2, part, 0)
@@ -207,14 +210,14 @@
         return move(ref, ref, c_send.at[g], c_recv.at[g], other)
 
     def w_step(s, _):
-        @pl.when(s < 5)
-        def _():
-            z_copy(s + 3).start()
-
-        @pl.when(s < 7)
-        def _():
-            z_copy(s + 1).wait_recv()
-            y_spread(s + 1, lambda zz, yy: wz.at[zz, yy])
+        @pl.when(s < 3)
+        def _():
+            z_copy(s + 5).start()
+
+        @pl.when(s < 6)
+        def _():
+            z_copy(s + 2).wait_recv()
+            y_spread(s + 2, lambda zz, yy: wz.at[zz, yy])
 
         @pl.when(s < 8)
         def _():
@@ -222,54 +225,54 @@
             for way in range(2):
                 x_copy(s, way).start()
 
-        pl.when(s == 0)(rows_first)
-
-        @pl.when(s < 5)
-        def _():
-            lax.fori_loop(3 * s, jnp.minimum(3 * s + 3, 14), rows_step, 0)
-
-        pl.when(s == 5)(rows_end)
-
-        @pl.when((s >= 1) & (s < 9))
-        def _():
-            for way in range(2):
-                x_copy(s - 1, way).wait_recv()
-                x_forward(s - 1, way).start()
+        for i in range(5):
+            pl.when(s == FIRST + i)(lambda i=i: first_step(i))
+
+        @pl.when((s >= RING) & (s < READY))
+        def _():
+            lax.fori_loop(SLOTS * (s - RING), jnp.minimum(SLOTS * (s - RING + 1), 14), rows_step, 0)
+
+        pl.when(s == READY)(rows_end)
 
         @pl.when((s >= 2) & (s < 10))
         def _():
             for way in range(2):
-                x_forward(s - 2, way).wait_recv()
-            core_copy(s - 2).start()
-
-        @pl.when((s >= 3) & (s < 11))
-        def _():
-            core_copy(s - 3).wait_recv()
-
-        @pl.when(s == 5)
-        def _():
-            lax.fori_loop(0, 3, multiply, 0)
-
-        @pl.when(s > 5)
-        def _():
-            multiply(s - 3, 0)
-
-        return 0
-
-    lax.fori_loop(0, 11, w_step, 0)
-
-    def activate(i, _):
-        spot = pl.ds(pl.multiple_of(i * 128, 128), 128)
-        gate, up = acc[spot, :F], acc[spot, F:]
-        value = (gate / (1.0 + jnp.exp(-gate)) * up).astype(BF16).reshape(8, ROWS, F)
-        hid[0, i] = value
-        hid[1, :, i] = value
-        return 0
-
-    lax.fori_loop(0, 8, activate, 0)
+                x_copy(s - 2, way).wait_recv()
+                x_forward(s - 2, way).start()
+
+        @pl.when((s >= 4) & (s < 12))
+        def _():
+            for way in range(2):
+                x_forward(s - 4, way).wait_recv()
+            core_copy(s - 4).start()
+
+        @pl.when(s >= 5)
+        def _():
+            core_copy(s - 5).wait_recv()
+            place(s - 5)
+
+        @pl.when(s == READY)
+        def _():
+            lax.fori_loop(0, READY - 4, multiply, 0)
+
+        @pl.when(s > READY)
+        def _():
+            multiply(s - 5, 0)
+
+        return 0
+
+    z_copy(1).wait_recv()
+    y_spread(1, lambda zz, yy: wz.at[zz, yy])
+    lax.fori_loop(0, 13, w_step, 0)
+
+    def activate(rows):
+        gate, up = rows[:, :F], rows[:, F:]
+        hid[...] = (gate / (1.0 + jnp.exp(-gate)) * up).astype(BF16)
 
     def term(half, index):
-        rows = hid[half, index].reshape(128, F)
+        pl.when(half == 0)(lambda: activate(acc[index].reshape(128, 2 * F)))
+        pl.when(half == 1)(lambda: activate(acc[:, index].reshape(128, 2 * F)))
+        rows = hid[...]
         scale = coef[half, index][:, :1]
         parts = [lax.dot_general(rows, wmat[half * 4 + i, :, 2 * F:], (((1,), (1,)), ((), ())),
                                  preferred_element_type=F32) for i in range(4)]
@@ -300,12 +303,8 @@
     lax.fori_loop(0, 2, begin, 0)
 
     def go(step, _):
-        def prepare(half, _):
-            for way in range(2):
-                terms[half, way] = term(half, mod(mine_of(half) + (1 - 2 * way) * (4 - step), 8))
-            return 0
-
-        lax.fori_loop(0, 2, prepare, 0)
+        def prepare(half, way):
+            terms[half, way] = term(half, mod(mine_of(half) + (1 - 2 * way) * (4 - step), 8))
 
         def pass_on(half, part, way, first):
             rows = rs_rows(way, part)
@@ -320,6 +319,7 @@
             def each(half, _):
                 for way in range(2):
                     if part == 0:
+                        prepare(half, way)
                         pl.when(step == 1)(lambda: pass_on(half, part, way, True))
                         pl.when(step > 1)(lambda: pass_on(half, part, way, False))
                     else:
@@ -356,23 +356,15 @@
     lax.fori_loop(0, 2, end, 0)
 
     for half in range(2):
-        ref = fin_recv.at[half, pl.ds(0, 7)]
-        move(ref, ref, fin_s.at[half], fin_r.at[half], right).wait_recv()
-        total = fin_recv[half, 0].astype(F32)
-        for i in range(1, 8):
-            total = total + fin_recv[half, i].astype(F32)
-        out_ref[:, half * HALF:(half + 1) * HALF] = total.astype(BF16)
-
-    move(xa.at[z, pl.ds(0, 7)], xa.at[z, pl.ds(0, 7)], sem_s1.at[0], sem_a1, right).wait_send()
-    move(xb.at[y, pl.ds(0, 7)], xb.at[y, pl.ds(0, 7)], sem_s1.at[1], sem_b1, right).wait_send()
+        for way in range(2):
+            for step in range(3 + (way == half)):
+                first(half, way, step).wait_send()
     for half in range(2):
         for way in range(2):
             rs_copy(half, way, 0, 1).wait_send()
             for step in range(1, 4):
                 for part in range(2):
                     rs_copy(half, way, step, part).wait_send()
-        ref = fin_send.at[half, pl.ds(0, 7)]
-        move(ref, ref, fin_s.at[half], fin_r.at[half], right).wait_send()
 
     def ring_drain(j, _):
         step = j // 4
@@ -398,6 +390,16 @@
         return 0
 
     lax.fori_loop(0, 8, drain, 0)
+
+    for half in range(2):
+        ref = fin_recv.at[half, pl.ds(0, 7)]
+        move(ref, ref, fin_s.at[half], fin_r.at[half], right).wait_recv()
+        total = fin_recv[half, 0].astype(F32)
+        for i in range(1, 8):
+            total = total + fin_recv[half, i].astype(F32)
+        out_ref[:, half * HALF:(half + 1) * HALF] = total.astype(BF16)
+        ref = fin_send.at[half, pl.ds(0, 7)]
+        move(ref, ref, fin_s.at[half], fin_r.at[half], right).wait_send()
 
 
 def per_device(tokens, norm_gain, expert_weights, slot_expert, pair_slots, combine_weights):
@@ -415,15 +417,15 @@
             pltpu.VMEM((NZ, NY, TILES, 4, 128), BF16),
             pltpu.VMEM((2, NX, NZ, NY, TILES, 4, 128), BF16),
             pltpu.VMEM((8, 256, 3 * F), BF16),
-            pltpu.VMEM((1024, 2 * F), F32),
-            pltpu.VMEM((2, 8, 8, ROWS, F), BF16),
+            pltpu.VMEM((8, 8, ROWS, 2 * F), F32),
+            pltpu.VMEM((128, F), BF16),
             pltpu.VMEM((2, 8, 128, 128), F32),
             pltpu.VMEM((2, 2, 128, HALF), F32),
             pltpu.VMEM((2, 2, 4, 128, HALF), BF16),
             pltpu.VMEM((2, 2, 4, 128, HALF), BF16),
             pltpu.VMEM((2, 8, ROWS, HALF), BF16),
             pltpu.VMEM((2, 8, ROWS, HALF), BF16),
-            sem, sem, sem((2,)), sem((64,)), sem((64,)), sem((8,)), sem((8,)), sem((8,)), sem((8,)), sem((8,)),
+            sem((16,)), sem((16,)), sem((64,)), sem((64,)), sem((8,)), sem((8,)), sem((8,)), sem((8,)), sem((8,)),
             sem((2, 8)), sem((2, 8)), sem((2, 8)), sem((2, 8)), sem((8,)), sem((8,)),
             sem((2, 2, 4, 2)), sem((2, 2, 4, 2)), sem((2,)), sem((2,)),
         ],

time: 133 us -> 127 us (0.955)
  Pallas kernels: 131 us -> 124 us
    pallas_call x1, Pallas kernels: 131 us -> 124 us  [per_device(): pl.pallas_call(kernel, out_shape=jax.ShapeDtypeStruct((ROWS, D), BF16), i...]
where the time goes in v3:
time: 127 us; the launch traced here: 126 us
  Pallas kernels  124 us (98%)
  local copies, waits for them, and re-layouts  1.47 us (1%)
    pallas_call x1, Pallas kernels, per_device(): pl.pallas_call(kernel, out_shape=jax.ShapeDtypeStruct((ROWS, D), BF16), i...  124 us

profile of v3, /device:TPU:6, one launch (start us, length us, event | category | flops | bytes accessed | tf_op | source)
XLA Modules:
  0.0 125.7 jit_solution(9688085848631308352)
XLA Ops:
  0.0 124.2 %shard_map.64 = bf16[16,2048]{1,0:T(8,128)(2,1)} custom-call(bf16[16,2048]{1,0:T(8,128)(2,1)} %tok_ref.1, f32[1,2048]{1,0:T(1,128)} %bitcast.8, bf16[64,18,4,128]{3,2,1,0:T(4,128)(2,1)} %bitcast.7, s32[1,128]{1,0:T(1,128)} %bitcast.11, s32[8,16]{1,0:T(8,128)} %bitcast.9, f32[8,16]{1,0:T(8,128)} %bitcast.10), custom_call_target="tpu_custom_call" | custom-call | tf_op jit(solution)/shard_map/pallas_call | solution.py:409
  124.2 1.5 %copy.8 = bf16[16,2048]{1,0:T(8,128)(2,1)} copy(bf16[16,2048]{1,0:T(8,128)(2,1)} %shard_map.64) | data formatting | bytes 131072

commit v4 on v3

--- a/solution.py
+++ b/solution.py
@@ -10,7 +10,7 @@
 HALF = D // 2
 TILES = 3 * F // 128
 BF16, F32 = jnp.bfloat16, jnp.float32
-FIRST, RING, READY, SLOTS = 0, 4, 9, 3
+FIRST, RING, READY, SLOTS = 0, 4, 11, 2
 
 
 def mod(value, size):
@@ -173,24 +173,20 @@
         def add(rows_of, first):
             column = pl.multiple_of((zz - first) * 256, 256)
 
-            def part(q, _):
-                rows = rows_of(q, column)
-                for n in range(3):
-                    at_n = slice(n * 512, (n + 1) * 512)
-                    part_of = jnp.dot(rows, wmat[zz, :, at_n], preferred_element_type=F32)
-                    acc[pl.ds(q * 4, 4), :, :, at_n] += part_of.reshape(4, 8, ROWS, 512)
-                return 0
-
-            lax.fori_loop(0, 2, part, 0)
+            rows = rows_of(column)
+            for n in range(3):
+                at_n = slice(n * 512, (n + 1) * 512)
+                part_of = jnp.dot(rows, wmat[zz, :, at_n], preferred_element_type=F32)
+                acc[:, :, :, at_n] += part_of.reshape(8, 8, ROWS, 512)
 
         @pl.when(zz < 4)
         def _():
-            add(lambda q, col: xa[pl.ds(q * 4, 4), :, :, pl.ds(col, 256)].reshape(512, 256), 0)
+            add(lambda col: xa[:, :, :, pl.ds(col, 256)].reshape(1024, 256), 0)
 
         @pl.when(zz >= 4)
         def _():
-            add(lambda q, col: jnp.concatenate(
-                [xb[:, q * 4 + i, :, pl.ds(col, 256)].reshape(128, 256) for i in range(4)], axis=0), 4)
+            add(lambda col: jnp.concatenate(
+                [xb[:, i, :, pl.ds(col, 256)].reshape(128, 256) for i in range(8)], axis=0), 4)
 
         return 0
 

time: 127 us -> 124 us (0.976); the launches traced: 126 us -> 124 us
    pallas_call x1, Pallas kernels: 124 us -> 123 us  [per_device(): pl.pallas_call(kernel, out_shape=jax.ShapeDtypeStruct((ROWS, D), BF16), i...]
where the time goes in v4:
time: 124 us
  Pallas kernels  123 us (99%)
  local copies, waits for them, and re-layouts  1.47 us (1%)
    pallas_call x1, Pallas kernels, per_device(): pl.pallas_call(kernel, out_shape=jax.ShapeDtypeStruct((ROWS, D), BF16), i...  123 us

profile of v4, /device:TPU:6, one launch (start us, length us, event | category | flops | bytes accessed | tf_op | source)
XLA Modules:
  0.0 124.2 jit_solution(11768313676826654384)
XLA Ops:
  0.0 122.7 %shard_map.64 = bf16[16,2048]{1,0:T(8,128)(2,1)} custom-call(bf16[16,2048]{1,0:T(8,128)(2,1)} %tok_ref.1, f32[1,2048]{1,0:T(1,128)} %bitcast.8, bf16[64,18,4,128]{3,2,1,0:T(4,128)(2,1)} %bitcast.7, s32[1,128]{1,0:T(1,128)} %bitcast.11, s32[8,16]{1,0:T(8,128)} %bitcast.9, f32[8,16]{1,0:T(8,128)} %bitcast.10), custom_call_target="tpu_custom_call" | custom-call | tf_op jit(solution)/shard_map/pallas_call | solution.py:405
  122.7 1.5 %copy.8 = bf16[16,2048]{1,0:T(8,128)(2,1)} copy(bf16[16,2048]{1,0:T(8,128)(2,1)} %shard_map.64) | data formatting | bytes 131072

commit v5 on v4

--- a/solution.py
+++ b/solution.py
@@ -230,36 +230,32 @@
 
         pl.when(s == READY)(rows_end)
 
-        @pl.when((s >= 2) & (s < 10))
-        def _():
-            for way in range(2):
-                x_copy(s - 2, way).wait_recv()
-                x_forward(s - 2, way).start()
-
-        @pl.when((s >= 4) & (s < 12))
-        def _():
-            for way in range(2):
-                x_forward(s - 4, way).wait_recv()
-            core_copy(s - 4).start()
-
-        @pl.when(s >= 5)
-        def _():
-            core_copy(s - 5).wait_recv()
-            place(s - 5)
+        @pl.when((s >= 1) & (s < 9))
+        def _():
+            for way in range(2):
+                x_copy(s - 1, way).wait_recv()
+                x_forward(s - 1, way).start()
+
+        @pl.when((s >= 3) & (s < 11))
+        def _():
+            for way in range(2):
+                x_forward(s - 3, way).wait_recv()
+            core_copy(s - 3).start()
+
+        @pl.when(s >= 4)
+        def _():
+            core_copy(s - 4).wait_recv()
+            place(s - 4)
 
         @pl.when(s == READY)
         def _():
-            lax.fori_loop(0, READY - 4, multiply, 0)
-
-        @pl.when(s > READY)
-        def _():
-            multiply(s - 5, 0)
+            lax.fori_loop(0, READY - 3, multiply, 0)
 
         return 0
 
     z_copy(1).wait_recv()
     y_spread(1, lambda zz, yy: wz.at[zz, yy])
-    lax.fori_loop(0, 13, w_step, 0)
+    lax.fori_loop(0, 12, w_step, 0)
 
     def activate(rows):
         gate, up = rows[:, :F], rows[:, F:]

time: 124 us -> 126 us (1.016)
  the two profiles are of different devices: /device:TPU:6 before, /device:TPU:4 now
where the time goes in v5:
time: 126 us; the launch traced here: 125 us
  Pallas kernels  124 us (98%)
  local copies, waits for them, and re-layouts  1.47 us (1%)
    pallas_call x1, Pallas kernels, per_device(): pl.pallas_call(kernel, out_shape=jax.ShapeDtypeStruct((ROWS, D), BF16), i...  124 us

profile of v5, /device:TPU:4, one launch (start us, length us, event | category | flops | bytes accessed | tf_op | source)
XLA Modules:
  0.0 125.4 jit_solution(17297062381531192362)
XLA Ops:
  0.0 123.9 %shard_map.64 = bf16[16,2048]{1,0:T(8,128)(2,1)} custom-call(bf16[16,2048]{1,0:T(8,128)(2,1)} %tok_ref.1, f32[1,2048]{1,0:T(1,128)} %bitcast.8, bf16[64,18,4,128]{3,2,1,0:T(4,128)(2,1)} %bitcast.7, s32[1,128]{1,0:T(1,128)} %bitcast.11, s32[8,16]{1,0:T(8,128)} %bitcast.9, f32[8,16]{1,0:T(8,128)} %bitcast.10), custom_call_target="tpu_custom_call" | custom-call | tf_op jit(solution)/shard_map/pallas_call | solution.py:401
  123.9 1.5 %copy.8 = bf16[16,2048]{1,0:T(8,128)(2,1)} copy(bf16[16,2048]{1,0:T(8,128)(2,1)} %shard_map.64) | data formatting | bytes 131072
